TPU v7x, 512 devices: a whole 4x4x16 slice. The times are simulated.
512 devices in a mesh: ray: 16 (over y, x_hi, core), cuts: 32 (over x_lo, z).
Axes of the slice: x: 4 (x_hi: 2, x_lo: 2; x = x_hi * 2 + x_lo), y: 4, z: 16, core: 2. Of those that a mesh axis runs over, the one named last changes fastest.
Arguments:
- initial: float32 [64, 64, 4096], P('cuts', 'ray'), may hold values from 0.5 to 1.5
- measured: float32 [16, 32, 64, 4096], P('ray', None, 'cuts'), may hold values from 38.4 to 115.2
- order: int32 [16], replicated, may hold values from 0 to 15, each once
- angle_index: int32 [16, 32], replicated, may hold values from 0 to 2999
Outputs:
- reconstruction: float32 [64, 64, 4096], P('cuts', 'ray')
Inputs may be any that keep to these rules, and one draw needn't show every extreme that they name: Each stored subset appears once; the first 2 entries are the subsets run, in order, and stored subset j is held by index j of ray.
All inputs are finite; a program needn't handle non-finite values.
Results may differ from a plain program's by a relative error of at most 0.0003.
Values sent between devices are 32-bit elements; how exact they have to be, the bound alone decides.
A program may use at most 64 MiB of HBM per device.

v0:
```python
import jax
import jax.numpy as jnp
from jax import lax
from jax.sharding import PartitionSpec as P

SUBSETS = 2
NANG = 3000
TV_ITERS = 2


TV_STEP = 0.05
TV_EPS = 0.5
angle_group = 2


def broadcast(value, axis, source):
    kept = jnp.where(lax.axis_index(axis) == source, value, 0).astype(value.dtype)
    return lax.psum(kept, axis)


def padded_2(block, sides, width):
    for axis, dim in sides:
        count = lax.axis_size(axis)
        forward = [(i, i + 1) for i in range(count - 1)]
        backward = [(target, source) for source, target in forward]
        low = lax.ppermute(
            lax.slice_in_dim(block, block.shape[dim] - width, None, axis=dim), axis, forward
        )
        high = lax.ppermute(lax.slice_in_dim(block, 0, width, axis=dim), axis, backward)
        block = jnp.concatenate([low, block, high], axis=dim)
    return block


def strip_geometry(angle_row, first_row, total_rows, strip_rows):
    slopes = -1.0 + (2.0 * angle_row.astype(jnp.float32) + 1.0) / NANG
    row_pos = (first_row + jnp.arange(strip_rows, dtype=jnp.int32)).astype(jnp.float32) - (
        total_rows - 1
    ) / 2.0
    spread = slopes[:, None] * row_pos[None, :]
    floor_part = jnp.floor(spread)
    return (floor_part.astype(jnp.int32), spread - floor_part)


def row_windows(padded, starts, width):

    def row_one_row(plane, start):
        return lax.dynamic_slice_in_dim(plane, start, width, 1)

    return jax.vmap(row_one_row, in_axes=(1, 0), out_axes=1)(padded, starts)


def plane_windows(plane, starts, width):

    def plane_one_row(start):
        return lax.dynamic_slice_in_dim(plane, start, width, 1)

    return jax.vmap(plane_one_row, out_axes=1)(starts)


def project_block(padded, shifts, fraction, margin, width):
    angle_count, rows = shifts.shape
    groups = angle_count // angle_group

    def project_one_angle(shift_row, frac_row):
        window = row_windows(padded, margin - shift_row - 1, width + 1)
        weight = frac_row[None, :, None]
        return jnp.sum((1.0 - weight) * window[:, :, 1:] + weight * window[:, :, :-1], axis=1)

    def one_group(pieces):
        return jax.vmap(project_one_angle)(pieces[0], pieces[1])

    result = lax.map(
        one_group,
        (shifts.reshape(groups, angle_group, rows), fraction.reshape(groups, angle_group, rows)),
    )
    return result.reshape(angle_count, padded.shape[0], width)


def back_block(res_padded, shifts, fraction, margin, width):
    angle_count, rows = shifts.shape
    groups = angle_count // angle_group
    slices = res_padded.shape[1]

    def back_one_angle(plane, shift_row, frac_row):
        window = plane_windows(plane, margin + shift_row, width + 1)
        weight = frac_row[None, :, None]
        return (1.0 - weight) * window[:, :, :-1] + weight * window[:, :, 1:]

    def add_group(summed, pieces):
        terms = jax.vmap(back_one_angle)(pieces[0], pieces[1], pieces[2])
        return (summed + jnp.sum(terms, axis=0), None)

    planes = res_padded.reshape((groups, angle_group) + res_padded.shape[1:])
    summed, _ = lax.scan(
        add_group,
        jnp.zeros((slices, rows, width), jnp.float32),
        (
            planes,
            shifts.reshape(groups, angle_group, rows),
            fraction.reshape(groups, angle_group, rows),
        ),
    )
    return summed


def tv_step(extended, first_row, first_slice, total_rows, total_slices):
    count_s, count_r, breadth = extended.shape
    row_ids = first_row + jnp.arange(count_r, dtype=jnp.int32)
    slice_ids = first_slice + jnp.arange(count_s, dtype=jnp.int32)
    row_in = (row_ids >= 0) & (row_ids < total_rows)
    slice_in = (slice_ids >= 0) & (slice_ids < total_slices)
    centre = extended[:-1, :-1]
    cell_in = slice_in[:-1, None] & row_in[None, :-1]
    valid_r = cell_in & row_in[None, 1:]
    valid_s = cell_in & slice_in[1:, None]
    step_r = jnp.where(valid_r[:, :, None], extended[:-1, 1:] - centre, 0.0)
    step_s = jnp.where(valid_s[:, :, None], extended[1:, :-1] - centre, 0.0)
    along_c = jnp.concatenate(
        [centre[:, :, 1:] - centre[:, :, :-1], jnp.zeros_like(centre[:, :, :1])], axis=2
    )
    step_c = jnp.where(cell_in[:, :, None], along_c, 0.0)
    magnitude = jnp.sqrt(step_s * step_s + step_r * step_r + step_c * step_c + TV_EPS * TV_EPS)
    flow_r = step_r / magnitude
    flow_s = step_s / magnitude
    flow_c = step_c / magnitude
    inner_c = flow_c[1:, 1:]
    spread = flow_r[1:, 1:] - flow_r[1:, :-1] + flow_s[1:, 1:] - flow_s[:-1, 1:]
    spread = spread + inner_c - jnp.pad(inner_c[:, :, :-1], ((0, 0), (0, 0), (1, 0)))
    return extended[1:-1, 1:-1] + TV_STEP * spread


def on_device(initial, measured, order, angle_index):
    slices, strip_rows, breadth = initial.shape
    ray_count = lax.axis_size("ray")
    cut_count = lax.axis_size("cuts")
    ray_place = lax.axis_index("ray")
    cut_place = lax.axis_index("cuts")
    total_rows = strip_rows * ray_count
    total_slices = slices * cut_count
    angle_total = angle_index.shape[1]
    margin = total_rows // 2 + 2
    stored = measured[0]
    current = initial
    for subset in range(SUBSETS):
        subset_slot = order[subset]
        shifts, fraction = strip_geometry(
            angle_index[subset_slot], ray_place * strip_rows, total_rows, strip_rows
        )
        padded = jnp.pad(current, ((0, 0), (0, 0), (margin, margin)))
        partial_value = project_block(padded, shifts, fraction, margin, breadth)
        totals = lax.psum(partial_value, "ray")
        residual = broadcast(stored - totals, "ray", subset_slot)
        res_padded = jnp.pad(residual, ((0, 0), (0, 0), (margin, margin)))
        current = current + back_block(res_padded, shifts, fraction, margin, breadth) / (
            total_rows * angle_total
        )
        for tv_turn in range(TV_ITERS):
            extended = padded_2(current, (("ray", 1), ("cuts", 0)), 1)
            current = tv_step(
                extended,
                ray_place * strip_rows - 1,
                cut_place * slices - 1,
                total_rows,
                total_slices,
            )
    return current


def solution(mesh):
    return jax.shard_map(
        on_device,
        mesh=mesh,
        in_specs=(P("cuts", "ray", None), P("ray", None, "cuts", None), P(), P()),
        out_specs=P("cuts", "ray", None),
        check_vma=False,
    )
```

profile of v0, /device:TPU:1, one launch (start us, length us, event | category | flops | bytes accessed | tf_op | source)
XLA Modules:
  0.0 1834.5 jit_solution(4133876965931125556)
XLA Ops:
  14.4 270.8 %while.65 = (s32[]{:T(128)}, f32[16,2,2,4096]{3,2,1,0:T(2,128)S(1)}, f32[16,2,4]{2,1,0:T(2,128)S(1)}, f32[2,4,4164]{2,0,1:T(2,128)S(1)}, s32[16,2,4]{2,1,0:T(2,128)S(1)}, /*index=5*/s32[]{:T(128)}, s32[]{:T(128)}, s32[]{:T(128)}) while((s32[]{:T(128)}, f32[16,2,2,4096]{3,2,1,0:T(2,128)S(1)}, f32[16,2,4]{2,1,0:T(2,128)S(1)}, ...), condition=%wide.region_2.3_spmd, body=%wide.region_0.2_spmd.sunk | while | flops 245828 | bytes 789350 | solution.py:72
  287.0 160.3 %all-reduce.21.cloned.1.call-done = f32[32,2,4096]{2,1,0:T(2,128)} async-done(((f32[32,2,4096]{2,1,0:T(2,128)}), f32[32,2,4096]{2,1,0:T(2,128)}) %all-reduce.21.cloned.1.call-update) | async-done | bytes 1048592 | tf_op jit(solution)/shard_map/psum | solution.py:151
  450.5 156.9 %all-reduce.23.cloned.1.call-done = f32[32,2,4096]{2,1,0:T(2,128)} async-done(((f32[32,2,4096]{2,1,0:T(2,128)}), f32[32,2,4096]{2,1,0:T(2,128)}) %all-reduce.23.cloned.1.call-update) | async-done | bytes 1048592 | tf_op jit(solution)/shard_map/psum | solution.py:18
  609.8 274.4 %while.69 = (s32[]{:T(128)}, f32[2,4,4096]{2,0,1:T(2,128)S(1)}, f32[16,2,4]{2,1,0:T(2,128)S(1)}, f32[16,2,2,4164]{3,2,1,0:T(2,128)S(1)}, s32[16,2,4]{2,1,0:T(2,128)S(1)}, /*index=5*/s32[]{:T(128)}, s32[]{:T(128)}, s32[]{:T(128)}) while((s32[]{:T(128)}, f32[2,4,4096]{2,0,1:T(2,128)S(1)}, f32[16,2,4]{2,1,0:T(2,128)S(1)}, ...), condition=%wide.region_7.8_spmd.clone, body=%wide.region_5.7_spmd.clone.sunk | while | flops 294981 | bytes 1250288 | solution.py:94
  627.1 16.3 while.74
  644.3 16.3 while.74
  661.4 16.3 while.74
  678.6 16.3 while.74
  695.7 16.3 while.74
  712.9 16.3 while.74
  730.0 16.3 while.74
  747.2 16.3 while.74
  764.3 16.3 while.74
  781.5 16.3 while.74
  815.8 16.3 while.74
  832.9 16.3 while.74
  850.1 16.3 while.74
  924.3 270.8 %while.67 = (s32[]{:T(128)}, f32[16,2,2,4096]{3,2,1,0:T(2,128)S(1)}, f32[16,2,4]{2,1,0:T(2,128)S(1)}, f32[2,4,4164]{2,0,1:T(2,128)S(1)}, s32[16,2,4]{2,1,0:T(2,128)S(1)}, /*index=5*/s32[]{:T(128)}, s32[]{:T(128)}, s32[]{:T(128)}) while((s32[]{:T(128)}, f32[16,2,2,4096]{3,2,1,0:T(2,128)S(1)}, f32[16,2,4]{2,1,0:T(2,128)S(1)}, ...), condition=%wide.region_10.11_spmd, body=%wide.region_8.10_spmd.sunk | while | flops 245828 | bytes 789350 | solution.py:72
  1196.8 154.4 %all-reduce.25.cloned.1.call-done = f32[32,2,4096]{2,1,0:T(2,128)} async-done(((f32[32,2,4096]{2,1,0:T(2,128)}), f32[32,2,4096]{2,1,0:T(2,128)}) %all-reduce.25.cloned.1.call-update) | async-done | bytes 1048592 | tf_op jit(solution)/shard_map/psum | solution.py:151
  1354.2 157.0 %all-reduce.27.cloned.1.call-done = f32[32,2,4096]{2,1,0:T(2,128)} async-done(((f32[32,2,4096]{2,1,0:T(2,128)}), f32[32,2,4096]{2,1,0:T(2,128)}) %all-reduce.27.cloned.1.call-update) | async-done | bytes 1048592 | tf_op jit(solution)/shard_map/psum | solution.py:18
  1513.6 274.4 %while.71 = (s32[]{:T(128)}, f32[2,4,4096]{2,0,1:T(2,128)S(1)}, f32[16,2,4]{2,1,0:T(2,128)S(1)}, f32[16,2,2,4164]{3,2,1,0:T(2,128)S(1)}, s32[16,2,4]{2,1,0:T(2,128)S(1)}, /*index=5*/s32[]{:T(128)}, s32[]{:T(128)}, s32[]{:T(128)}) while((s32[]{:T(128)}, f32[2,4,4096]{2,0,1:T(2,128)S(1)}, f32[16,2,4]{2,1,0:T(2,128)S(1)}, ...), condition=%wide.region_15.16_spmd.clone, body=%wide.region_13.15_spmd.clone.sunk | while | flops 294981 | bytes 1250288 | solution.py:94
  1513.8 16.3 while.75
  1548.1 16.3 while.75
  1565.2 16.3 while.75
  1582.4 16.3 while.75
  1616.7 16.3 while.75
  1633.8 16.3 while.75
  1651.0 16.3 while.75
  1685.3 16.3 while.75
  1702.4 16.3 while.75
  1719.6 16.3 while.75
  1736.7 16.3 while.75
  (2230 shorter events, 1824.9 us)
Async XLA Ops:
  6.5 440.8 %all-reduce.21.cloned.1.call-start = ((), (), s32[]{:S(2)}) async-start(), calls=%async_computation | async-start | bytes 2097152 | tf_op jit(solution)/shard_map/psum | solution.py:151
  285.2 1.0 copy-start.1
  285.2 162.1 %copy-start = (f32[1,32,2,4096]{3,2,1,0:T(2,128)S(1)}, f32[1,32,2,4096]{3,2,1,0:T(2,128)}, u32[]{:S(2)}) copy-start(f32[1,32,2,4096]{3,2,1,0:T(2,128)} %param.13) | copy-start | bytes 3145732
  286.2 321.2 %all-reduce.23.cloned.1.call-start = ((), (), s32[]{:S(2)}) async-start(), calls=%async_computation.1 | async-start | bytes 2097152 | tf_op jit(solution)/shard_map/psum | solution.py:18
  450.2 901.0 %all-reduce.25.cloned.1.call-start = ((), (), s32[]{:S(2)}) async-start(), calls=%async_computation.2 | async-start | bytes 2097152 | tf_op jit(solution)/shard_map/psum | solution.py:151
  609.8 274.4 %copy-start.3 = (f32[2,4,4096]{2,1,0:T(4,128)S(1)}, f32[2,4,4096]{2,1,0:T(4,128)}, u32[]{:S(2)}) copy-start(f32[2,4,4096]{2,1,0:T(4,128)} %param.12) | copy-start | bytes 393220
  884.4 4.9 collective-permute-start
  886.3 6.7 collective-permute-start.1
  893.2 5.1 collective-permute-start.2
  896.4 5.7 collective-permute-start.3
  903.0 5.3 collective-permute-start.4
  906.4 6.7 collective-permute-start.5
  913.2 5.1 collective-permute-start.6
  916.4 6.3 collective-permute-start.7
  1195.2 1.0 copy-start.2
  1196.2 315.0 %all-reduce.27.cloned.1.call-start = ((), (), s32[]{:S(2)}) async-start(), calls=%async_computation.3 | async-start | bytes 2097152 | tf_op jit(solution)/shard_map/psum | solution.py:18
  1788.2 4.8 collective-permute-start.8
  1790.1 6.7 collective-permute-start.9
  1797.0 5.1 collective-permute-start.10
  1800.1 5.7 collective-permute-start.11
  1806.8 5.3 collective-permute-start.12
  1810.1 6.7 collective-permute-start.13
  1817.0 5.1 collective-permute-start.14
  1820.2 6.3 collective-permute-start.15
Sparse Core Ops, SparseCore 0:
  286.3 160.9 all-reduce.20
  450.5 156.8 all-reduce.22
  1196.3 154.8 all-reduce.24
  1354.3 156.8 all-reduce.26
where the time goes:
time: 1850 us; the launch traced here: 1830 us
  local copies, waits for them, and re-layouts  1050 us (57%)
  waiting for transfers between devices  664 us (36%)
  other arithmetic  47.8 us (3%)
  starting transfers between devices  38.2 us (2%)
  between operations  18.7 us (1%)
    gather x1536, local copies, waits for them, and re-layouts  1030 us
    psum x2, waiting for transfers between devices, on_device(): totals = lax.psum(partial_value, 'ray')  315 us
    psum x2, waiting for transfers between devices, broadcast(): return lax.psum(kept, axis)  314 us
  transfers between devices with their start and end apart: 20, of which 16 were waited for; matrix products, arithmetic and copies ran while one was open for 0% of the time, Pallas kernels for 0%

commit v1 on v0

v1 whole, which is shorter than its diff:
```python
import functools

import jax
import jax.numpy as jnp
from jax import lax
from jax.experimental import pallas as pl
from jax.experimental.pallas import tpu as pltpu
from jax.sharding import PartitionSpec as P

SUBSETS = 2
NANG = 3000
TV_ITERS = 2
TV_STEP = 0.05
TV_EPS = 0.5
MESH = pl.DeviceIdType.MESH
LANE = 128


def split(value):
    high = value.astype(jnp.bfloat16)
    return high, (value - high.astype(jnp.float32)).astype(jnp.bfloat16)


def dot3(left_hi, left_lo, right):
    right_hi, right_lo = split(right)
    dot = functools.partial(jnp.dot, preferred_element_type=jnp.float32)
    return dot(left_hi, right_hi) + dot(left_lo, right_hi) + dot(left_hi, right_lo)


def kernel(
    rays, cuts,
    init_ref, meas_ref, order_ref, angle_ref, out_ref,
    xin, mall, xw, kf_hi, kf_lo, kb_hi, kb_lo, ext, zland, hland, obuf,
    x_send, x_recv, m_send, m_recv, z_send, z_recv, h_send, h_recv, o_send, o_recv, own_sem,
):
    slices, strip, breadth = init_ref.shape
    angles = meas_ref.shape[1]
    rows = strip * rays
    chunk = breadth // rays
    reach = chunk + 2 * LANE
    me = lax.axis_index("ray")
    cut = lax.axis_index("cuts")
    up, down = lax.rem(cut + 1, cuts), lax.rem(cut + cuts - 1, cuts)
    east, west = lax.rem(me + 1, rays), lax.rem(me + rays - 1, rays)

    barrier = pltpu.get_barrier_semaphore()

    def greet(step, carry):
        peer = lax.rem(me + step, rays)
        pl.semaphore_signal(barrier, inc=1, device_id=(peer, cut), device_id_type=MESH)
        return carry

    lax.fori_loop(1, rays, greet, 0)
    for near in (up, down):
        pl.semaphore_signal(barrier, inc=1, device_id=(me, near), device_id_type=MESH)
    pl.semaphore_wait(barrier, rays + 1)

    def window(place):
        start = jnp.clip(place * chunk - LANE, 0, breadth - reach)
        offset = start - place * chunk + 2 * LANE
        return pl.multiple_of(start, LANE), pl.multiple_of(offset, LANE)

    def x_copy(peer):
        start, offset = window(peer)
        return pltpu.make_async_remote_copy(
            src_ref=init_ref.at[:, :, pl.ds(start, reach)],
            dst_ref=xin.at[me, :, :, pl.ds(offset, reach)],
            send_sem=x_send.at[peer],
            recv_sem=x_recv.at[me],
            device_id=(peer, cut),
            device_id_type=MESH,
        )

    def x_arrival(peer):
        start, offset = window(me)
        return pltpu.make_async_remote_copy(
            src_ref=init_ref.at[:, :, pl.ds(start, reach)],
            dst_ref=xin.at[peer, :, :, pl.ds(offset, reach)],
            send_sem=x_send.at[peer],
            recv_sem=x_recv.at[peer],
            device_id=(peer, cut),
            device_id_type=MESH,
        )

    def m_copy(peer, s):
        start, offset = window(peer)
        return pltpu.make_async_remote_copy(
            src_ref=meas_ref.at[0, :, s, pl.ds(start, reach)],
            dst_ref=mall.at[me, s, :, pl.ds(offset, reach)],
            send_sem=m_send.at[s, peer],
            recv_sem=m_recv.at[s, me],
            device_id=(peer, cut),
            device_id_type=MESH,
        )

    def m_arrival(peer, s):
        start, offset = window(me)
        return pltpu.make_async_remote_copy(
            src_ref=meas_ref.at[0, :, s, pl.ds(start, reach)],
            dst_ref=mall.at[peer, s, :, pl.ds(offset, reach)],
            send_sem=m_send.at[s, peer],
            recv_sem=m_recv.at[s, peer],
            device_id=(peer, cut),
            device_id_type=MESH,
        )

    def each_peer(action):
        def body(step, carry):
            action(lax.rem(me + step, rays))
            return carry

        lax.fori_loop(1, rays, body, 0)

    each_peer(lambda peer: x_copy(peer).start())

    def start_m(peer):
        for s in range(slices):
            m_copy(peer, s).start()

    each_peer(start_m)
    start, offset = window(me)
    own = [
        pltpu.make_async_copy(
            init_ref.at[:, :, pl.ds(start, reach)],
            xin.at[me, :, :, pl.ds(offset, reach)],
            own_sem.at[0],
        )
    ]
    for s in range(slices):
        own.append(
            pltpu.make_async_copy(
                meas_ref.at[0, :, s, pl.ds(start, reach)],
                mall.at[me, s, :, pl.ds(offset, reach)],
                own_sem.at[1 + s],
            )
        )
    for copy in own:
        copy.start()

    def iota(shape, dim):
        return lax.broadcasted_iota(jnp.int32, shape, dim)

    def geometry(subset):
        slot = order_ref[subset]
        picked = angle_ref[pl.ds(slot, 1), :].astype(jnp.float32)
        slope_row = -1.0 + (2.0 * picked + 1.0) / NANG
        wide = jnp.broadcast_to(slope_row, (angles, angles))
        eye = iota((angles, angles), 0) == iota((angles, angles), 1)
        slope_col = jnp.sum(jnp.where(eye, wide, 0.0), axis=1, keepdims=True)
        half = rows // 2
        taps_f = 4
        groups_f = kf_hi.shape[1] // angles
        lane = iota((angles, taps_f * rows), 1)
        position = (lane % rows).astype(jnp.float32) - (rows - 1) / 2.0
        spread = slope_col * position
        tap = lane // rows - half
        for group in range(groups_f):
            place = (tap + taps_f * group).astype(jnp.float32)
            hat = jnp.maximum(1.0 - jnp.abs(place - spread), 0.0)
            high, low = split(hat)
            kf_hi[subset, pl.ds(group * angles, angles), :] = high
            kf_lo[subset, pl.ds(group * angles, angles), :] = low
        taps_b = kb_hi.shape[2] // angles
        groups_b = kb_hi.shape[1] // rows
        slope_wide = jnp.concatenate([slope_row] * taps_b, axis=1)
        lane = iota((rows, taps_b * angles), 1)
        position = iota((rows, taps_b * angles), 0).astype(jnp.float32) - (rows - 1) / 2.0
        spread = slope_wide * position
        tap = lane // angles - half
        for group in range(groups_b):
            place = (tap + taps_b * group).astype(jnp.float32)
            hat = jnp.maximum(1.0 - jnp.abs(place - spread), 0.0)
            high, low = split(hat)
            kb_hi[subset, pl.ds(group * rows, rows), :] = high
            kb_lo[subset, pl.ds(group * rows, rows), :] = low

    for subset in range(SUBSETS):
        geometry(subset)

    own[0].wait()
    each_peer(lambda peer: x_arrival(peer).wait_recv())

    column = iota((rows, reach), 1) + me * chunk - LANE
    inside = (column >= 0) & (column < breadth)
    bin_place = iota((angles, reach), 1) + me * chunk - LANE
    bin_inside = (bin_place >= 0) & (bin_place < breadth)
    for s in range(slices):
        for p in range(rays):
            xw[s, p * strip:(p + 1) * strip, :] = xin[p, s, :, LANE:LANE + reach]
    for s in range(slices):
        xw[s] = jnp.where(inside, xw[s], 0.0)

    ring = chunk + LANE
    half_lane = iota((1, LANE), 1) < LANE // 2

    def circle(value):
        edge = jnp.where(half_lane, value[:, reach - LANE:], value[:, :LANE])
        return jnp.concatenate([value[:, LANE:LANE + chunk], edge], axis=1)

    def turn(value, amount):
        amount = amount % value.shape[1]
        return value if amount == 0 else pltpu.roll(value, amount, 1)

    def project_back(subset, s, slot):
        half = rows // 2
        current = xw[s]
        taps = kf_hi.shape[2] // rows
        stacked = jnp.concatenate([turn(current, j) for j in range(taps)], axis=0)
        lines = dot3(kf_hi[subset], kf_lo[subset], stacked)
        forward = jnp.zeros((angles, reach), jnp.float32)
        for group in range(lines.shape[0] // angles):
            forward += turn(lines[group * angles:(group + 1) * angles], taps * group - half)
        stored = mall[slot, s, :, LANE:LANE + reach]
        residual = circle(jnp.where(bin_inside, stored - forward, 0.0))
        taps = kb_hi.shape[2] // angles
        stacked = jnp.concatenate([turn(residual, -j) for j in range(taps)], axis=0)
        lines = dot3(kb_hi[subset], kb_lo[subset], stacked)
        back = jnp.zeros((rows, ring), jnp.float32)
        for group in range(lines.shape[0] // rows):
            back += turn(lines[group * rows:(group + 1) * rows], half - taps * group)
        return circle(current) + back / (rows * angles)

    ring_lane = iota((rows, ring), 1)
    ring_column = me * chunk + jnp.where(ring_lane < chunk + LANE // 2, ring_lane, ring_lane - ring)
    valid_c = (ring_column >= 0) & (ring_column < breadth - 1)
    valid_r = iota((rows, ring), 0) < rows - 1
    first_slice = cut * slices - 2
    total_slices = slices * cuts

    def tv_pass(source, target, low, high):
        flow_s_before = None
        for t in range(low - 1, high):
            centre = ext[source, t]
            step_s = ext[source, t + 1] - centre
            place = first_slice + t
            step_s = jnp.where((place >= 0) & (place < total_slices - 1), step_s, 0.0)
            step_r = jnp.where(valid_r, pltpu.roll(centre, rows - 1, 0) - centre, 0.0)
            step_c = jnp.where(valid_c, turn(centre, -1) - centre, 0.0)
            inverse = lax.rsqrt(
                step_s * step_s + step_r * step_r + step_c * step_c + TV_EPS * TV_EPS
            )
            flow_s = step_s * inverse
            if t >= low:
                flow_r = step_r * inverse
                flow_c = step_c * inverse
                spread = flow_s - flow_s_before
                spread = spread + flow_r - pltpu.roll(flow_r, 1, 0)
                spread = spread + flow_c - turn(flow_c, 1)
                ext[target, t] = centre + TV_STEP * spread
            flow_s_before = flow_s

    for subset in range(SUBSETS):
        slot = order_ref[subset]
        if subset == 0:
            for copy in own[1:]:
                copy.wait()

            def arrived(peer):
                for s in range(slices):
                    m_arrival(peer, s).wait_recv()

            each_peer(arrived)
        for s in range(slices):
            ext[0, 2 + s] = project_back(subset, s, slot)
        copies = [
            pltpu.make_async_remote_copy(
                src_ref=ext.at[0, pl.ds(2, slices)],
                dst_ref=zland.at[subset, side],
                send_sem=z_send.at[subset, side],
                recv_sem=z_recv.at[subset, side],
                device_id=(me, near),
                device_id_type=MESH,
            )
            for side, near in ((0, up), (1, down))
        ]
        for copy in copies:
            copy.start()
        for copy in copies:
            copy.wait()
        for s in range(slices):
            ext[0, s] = zland[subset, 0, s]
            ext[0, 2 + slices + s] = zland[subset, 1, s]
        tv_pass(0, 1, 1, 3 + slices)
        tv_pass(1, 0, 2, 2 + slices)
        if subset < SUBSETS - 1:
            copies = [
                pltpu.make_async_remote_copy(
                    src_ref=ext.at[0, pl.ds(2, slices), :, pl.ds(lane, LANE)],
                    dst_ref=hland.at[side],
                    send_sem=h_send.at[side],
                    recv_sem=h_recv.at[side],
                    device_id=(near, cut),
                    device_id_type=MESH,
                )
                for side, near, lane in ((0, east, chunk - LANE), (1, west, 0))
            ]
            for copy in copies:
                copy.start()
            for copy in copies:
                copy.wait()
            for s in range(slices):
                joined = jnp.concatenate(
                    [hland[0, s], ext[0, 2 + s, :, :chunk], hland[1, s]], axis=1
                )
                xw[s] = jnp.where(inside, joined, 0.0)

    for s in range(slices):
        for p in range(rays):
            obuf[p, s] = ext[0, 2 + s, p * strip:(p + 1) * strip, :chunk]

    def o_copy(peer):
        return pltpu.make_async_remote_copy(
            src_ref=obuf.at[peer],
            dst_ref=out_ref.at[:, :, pl.ds(pl.multiple_of(me * chunk, LANE), chunk)],
            send_sem=o_send.at[peer],
            recv_sem=o_recv.at[me],
            device_id=(peer, cut),
            device_id_type=MESH,
        )

    def o_arrival(peer):
        return pltpu.make_async_remote_copy(
            src_ref=obuf.at[peer],
            dst_ref=out_ref.at[:, :, pl.ds(pl.multiple_of(peer * chunk, LANE), chunk)],
            send_sem=o_send.at[peer],
            recv_sem=o_recv.at[peer],
            device_id=(peer, cut),
            device_id_type=MESH,
        )

    each_peer(lambda peer: o_copy(peer).start())
    mine = pltpu.make_async_copy(
        obuf.at[me], out_ref.at[:, :, pl.ds(pl.multiple_of(me * chunk, LANE), chunk)], own_sem.at[0]
    )
    mine.start()
    each_peer(lambda peer: o_arrival(peer).wait_recv())
    mine.wait()

    def sent(peer):
        x_copy(peer).wait_send()
        for s in range(slices):
            m_copy(peer, s).wait_send()
        o_copy(peer).wait_send()

    each_peer(sent)


def on_device(rays, cuts, initial, measured, order, angle_index):
    slices, strip, breadth = initial.shape
    angles = measured.shape[1]
    rows = strip * rays
    chunk = breadth // rays
    reach = chunk + 2 * LANE
    ring = chunk + LANE
    taps_f, taps_b = 4, 8
    groups_f = -(-(rows + 1) // taps_f)
    groups_b = -(-(rows + 1) // taps_b)
    dma = pltpu.SemaphoreType.DMA
    f32, bf16 = jnp.float32, jnp.bfloat16
    return pl.pallas_call(
        functools.partial(kernel, rays, cuts),
        out_shape=jax.ShapeDtypeStruct(initial.shape, f32),
        in_specs=[
            pl.BlockSpec(memory_space=pl.ANY),
            pl.BlockSpec(memory_space=pl.ANY),
            pl.BlockSpec(memory_space=pltpu.SMEM),
            pl.BlockSpec(memory_space=pltpu.VMEM),
        ],
        out_specs=pl.BlockSpec(memory_space=pl.ANY),
        scratch_shapes=[
            pltpu.VMEM((rays, slices, strip, reach + 2 * LANE), f32),
            pltpu.VMEM((rays, slices, angles, reach + 2 * LANE), f32),
            pltpu.VMEM((slices, rows, reach), f32),
            pltpu.VMEM((SUBSETS, groups_f * angles, taps_f * rows), bf16),
            pltpu.VMEM((SUBSETS, groups_f * angles, taps_f * rows), bf16),
            pltpu.VMEM((SUBSETS, groups_b * rows, taps_b * angles), bf16),
            pltpu.VMEM((SUBSETS, groups_b * rows, taps_b * angles), bf16),
            pltpu.VMEM((2, slices + 4, rows, ring), f32),
            pltpu.VMEM((SUBSETS, 2, slices, rows, ring), f32),
            pltpu.VMEM((2, slices, rows, LANE), f32),
            pltpu.VMEM((rays, slices, strip, chunk), f32),
            dma((rays,)), dma((rays,)),
            dma((slices, rays)), dma((slices, rays)),
            dma((SUBSETS, 2)), dma((SUBSETS, 2)),
            dma((2,)), dma((2,)),
            dma((rays,)), dma((rays,)),
            dma((1 + slices,)),
        ],
        compiler_params=pltpu.CompilerParams(
            collective_id=0, has_side_effects=True, vmem_limit_bytes=50 * 2**20
        ),
    )(initial, measured, order, angle_index)


def solution(mesh):
    return jax.shard_map(
        functools.partial(on_device, mesh.shape["ray"], mesh.shape["cuts"]),
        mesh=mesh,
        in_specs=(P("cuts", "ray", None), P("ray", None, "cuts", None), P(), P()),
        out_specs=P("cuts", "ray", None),
        check_vma=False,
    )
```

time: 1850 us -> 80 us (0.04)
  local copies, waits for them, and re-layouts: 1050 us -> 4.14 us
  waiting for transfers between devices: 664 us -> 0 us
  Pallas kernels: 0 us -> 75.6 us
  other arithmetic: 47.8 us -> 0 us
  starting transfers between devices: 38.2 us -> 0 us
  between operations: 18.7 us -> 0.01 us
    gather x1600 -> x0, local copies, waits for them, and re-layouts: 1040 us -> none
    psum x4 -> x0, waiting for transfers between devices: 629 us -> none  [the longest x2 315 us: on_device(): totals = lax.psum(partial_value, 'ray')]
    pallas_call x0 -> x1, Pallas kernels: none -> 75.6 us  [on_device(): pl.pallas_call(functools.partial(kernel, rays, cuts), out_shape=jax.Shape...]
    ppermute x16 -> x0, starting transfers between devices: 38 us -> none  [the longest x8 23.3 us: padded_2(): lax.ppermute(lax.slice_in_dim(block, block.shape[dim] - width, None, axis...]
    ppermute x16 -> x0, waiting for transfers between devices: 34.9 us -> none  [the longest x8 32.4 us: padded_2(): lax.ppermute(lax.slice_in_dim(block, 0, width, axis=dim), axis, backward)]
    reduce_sum x64 -> x0, other arithmetic: 28.6 us -> none  [the longest x32 15.1 us: add_group(): return (summed + jnp.sum(terms, axis=0), None)]
  transfers between devices with their start and end apart: 20 -> 0, of which waited for: 16 -> 0; matrix products, arithmetic and copies ran while one was open for 0% -> 0% of each run, Pallas kernels for 0% -> 0%
where the time goes in v1:
time: 80 us; the launch traced here: 79.8 us
  Pallas kernels  75.6 us (94%)
  local copies, waits for them, and re-layouts  4.14 us (5%)
    pallas_call x1, Pallas kernels, on_device(): pl.pallas_call(functools.partial(kernel, rays, cuts), out_shape=jax.Shape...  75.6 us
    unnamed x9, local copies, waits for them, and re-layouts  4.14 us

profile of v1, /device:TPU:1, one launch (start us, length us, event | category | flops | bytes accessed | tf_op | source)
XLA Modules:
  0.0 79.8 jit_solution(1113081578851552954)
XLA Ops:
  0.0 0.0 copy-start
  0.0 1.2 %copy-done = f32[1,32,2,4096]{3,2,1,0:T(2,128)S(1)} copy-done((f32[1,32,2,4096]{3,2,1,0:T(2,128)S(1)}, f32[1,32,2,4096]{3,2,1,0:T(2,128)}, u32[]{:S(2)}) %copy-start) | copy-done | bytes 1048600
  1.2 0.0 copy-start.1
  1.2 0.9 %copy-done.1 = f32[2,4,4096]{2,1,0:T(4,128)S(1)} copy-done((f32[2,4,4096]{2,1,0:T(4,128)S(1)}, f32[2,4,4096]{2,1,0:T(4,128)}, u32[]{:S(2)}) %copy-start.1) | copy-done | bytes 131096
  2.1 0.0 copy-start.2
  2.1 0.7 copy-done.2
  2.8 0.0 copy-start.3
  2.8 0.7 copy-done.3
  3.5 75.6 %shard_map.46 = f32[2,4,4096]{2,1,0:T(4,128)S(1)} custom-call(f32[2,4,4096]{2,1,0:T(4,128)S(1)} %copy-done.1, f32[1,32,2,4096]{3,2,1,0:T(2,128)S(1)} %copy-done, s32[16]{0:T(128)S(1)} %copy-done.3, s32[16,32]{1,0:T(8,128)S(1)} %copy-done.2), custom_call_target="tpu_custom_call" | custom-call | tf_op jit(solution)/shard_map/pallas_call | solution.py:360
  79.1 0.7 copy.6
Async XLA Ops:
  0.0 1.2 %copy-start = (f32[1,32,2,4096]{3,2,1,0:T(2,128)S(1)}, f32[1,32,2,4096]{3,2,1,0:T(2,128)}, u32[]{:S(2)}) copy-start(f32[1,32,2,4096]{3,2,1,0:T(2,128)} %meas_ref.1) | copy-start | bytes 3145732
  1.2 0.9 %copy-start.1 = (f32[2,4,4096]{2,1,0:T(4,128)S(1)}, f32[2,4,4096]{2,1,0:T(4,128)}, u32[]{:S(2)}) copy-start(f32[2,4,4096]{2,1,0:T(4,128)} %init_ref.1) | copy-start | bytes 393220
  2.1 0.7 copy-start.2
  2.8 0.7 copy-start.3

commit v2 on v1

v2 whole, which is shorter than its diff:
```python
import functools

import jax
import jax.numpy as jnp
from jax import lax
from jax.experimental import pallas as pl
from jax.experimental.pallas import tpu as pltpu
from jax.sharding import PartitionSpec as P

SUBSETS = 2
NANG = 3000
TV_ITERS = 2
TV_STEP = 0.05
TV_EPS = 0.5
MESH = pl.DeviceIdType.MESH
LANE = 128


def split(value):
    high = value.astype(jnp.bfloat16)
    return high, (value - high.astype(jnp.float32)).astype(jnp.bfloat16)


dot = functools.partial(jnp.dot, preferred_element_type=jnp.float32)


def dot2(left, right):
    right_hi, right_lo = split(right)
    return dot(left, right_hi) + dot(left, right_lo)


def dot3(left_hi, left_lo, right):
    right_hi, right_lo = split(right)
    return dot(left_hi, right_hi) + dot(left_lo, right_hi) + dot(left_hi, right_lo)


def band_rows(rows, taps):
    half = rows // 2
    kept = []
    for group in range(-(-(rows + 1) // taps)):
        first = taps * group - half
        nearest = min(abs(first + j) for j in range(taps))
        ends = sum(1 for i in range(half) if half - 0.5 - i > nearest - 1)
        kept.append(min(half, -(-ends // 8) * 8))
    return kept


FAR_FIRST = (10, 11, 14, 15, 6, 7, 8, 9, 2, 3, 12, 13, 4, 5, 1)


def partner(me, mask):
    return sum(
        bit * (1 - (me // bit) % 2 if mask & bit else (me // bit) % 2) for bit in (1, 2, 4, 8)
    )


def chunk_of(ray):
    core, high, y = ray % 2, (ray // 2) % 2, ray // 4
    return 2 * (y + high * (7 - 2 * y)) + core


def ray_of(chunk):
    core, spot = chunk % 2, chunk // 2
    high = spot // 4
    y = spot + high * (7 - 2 * spot)
    return (y * 2 + high) * 2 + core


def kernel(
    rays, cuts,
    init_ref, meas_ref, order_in, angle_in, out_ref,
    order_ref, angle_ref, mv, xin, m_mid, m_all, m_edge, xw, kf, kb_hi, kb_lo,
    ext, pack, zland, pland, hland, obuf,
    x_send, x_recv, a_send, a_recv, z_send, z_recv, p_send, p_recv,
    h_send, h_recv, e_send, e_recv, o_send, o_recv, own_sem,
):
    slices, strip, breadth = init_ref.shape
    angles = meas_ref.shape[1]
    rows = strip * rays
    chunk = breadth // rays
    reach = chunk + 2 * LANE
    ring = chunk + LANE
    me = lax.axis_index("ray")
    cut = lax.axis_index("cuts")
    place = chunk_of(me)
    up, down = lax.rem(cut + 1, cuts), lax.rem(cut + cuts - 1, cuts)
    east, west = ray_of(lax.rem(place + 1, rays)), ray_of(lax.rem(place + rays - 1, rays))
    peers = [partner(me, mask) for mask in FAR_FIRST]

    barrier = pltpu.get_barrier_semaphore()
    for peer in peers:
        pl.semaphore_signal(barrier, inc=1, device_id=(peer, cut), device_id_type=MESH)
    for near in (up, down):
        pl.semaphore_signal(barrier, inc=1, device_id=(me, near), device_id_type=MESH)

    def window(spot):
        start = jnp.clip(spot * chunk - LANE, 0, breadth - reach)
        offset = start - spot * chunk + 2 * LANE
        return pl.multiple_of(start, LANE), pl.multiple_of(offset, LANE)

    local = [
        pltpu.make_async_copy(order_in, order_ref, own_sem.at[0]),
        pltpu.make_async_copy(angle_in, angle_ref, own_sem.at[1]),
    ]
    start, offset = window(place)
    mine = pltpu.make_async_copy(
        init_ref.at[:, :, pl.ds(start, reach)],
        xin.at[me, :, :, pl.ds(offset, reach)],
        own_sem.at[2],
    )
    held = [
        pltpu.make_async_copy(meas_ref.at[0, :, s], mv.at[s], own_sem.at[3 + s])
        for s in range(slices)
    ]
    for copy in [*local, *held, mine]:
        copy.start()

    def send(src, dst, send_sem, recv_sem, target):
        return pltpu.make_async_remote_copy(
            src_ref=src, dst_ref=dst, send_sem=send_sem, recv_sem=recv_sem,
            device_id=target, device_id_type=MESH,
        )

    def x_copy(peer, arriving):
        start, offset = window(place if arriving else chunk_of(peer))
        origin = peer if arriving else me
        return send(
            init_ref.at[:, :, pl.ds(start, reach)],
            xin.at[origin, :, :, pl.ds(offset, reach)],
            x_send.at[peer], x_recv.at[origin], (peer, cut),
        )

    def a_copy(peer, arriving):
        column = pl.multiple_of(chunk * (place if arriving else chunk_of(peer)), chunk)
        origin = peer if arriving else me
        return send(
            mv.at[:, :, pl.ds(column, chunk)], m_all.at[origin],
            a_send.at[peer], a_recv.at[origin], (peer, cut),
        )

    def o_copy(peer, arriving):
        column = pl.multiple_of(chunk * (chunk_of(peer) if arriving else place), chunk)
        origin = peer if arriving else me
        return send(
            obuf.at[peer], out_ref.at[:, :, pl.ds(column, chunk)],
            o_send.at[peer], o_recv.at[origin], (peer, cut),
        )

    def iota(shape, dim):
        return lax.broadcasted_iota(jnp.int32, shape, dim)

    half = rows // 2
    taps_f = kf.shape[2] // rows
    taps_b = kb_hi.shape[2] // angles
    bands = band_rows(rows, taps_b)

    def geometry(subset):
        slot = order_ref[subset]
        picked = angle_ref[pl.ds(slot, 1), :].astype(jnp.float32)
        slope_row = -1.0 + (2.0 * picked + 1.0) / NANG
        wide = jnp.broadcast_to(slope_row, (angles, angles))
        eye = iota((angles, angles), 0) == iota((angles, angles), 1)
        slope_col = jnp.sum(jnp.where(eye, wide, 0.0), axis=1, keepdims=True)
        lane = iota((angles, taps_f * rows), 1)
        position = (lane % rows).astype(jnp.float32) - (rows - 1) / 2.0
        spread = jnp.floor(slope_col * position * 256.0 + 0.5) / 256.0
        tap = lane // rows - half
        for group in range(kf.shape[1] // angles):
            reached = (tap + taps_f * group).astype(jnp.float32)
            hat = jnp.maximum(1.0 - jnp.abs(reached - spread), 0.0)
            kf[subset, group * angles:(group + 1) * angles, :] = hat.astype(jnp.bfloat16)
        slope_wide = jnp.concatenate([slope_row] * taps_b, axis=1)
        lane = iota((rows, taps_b * angles), 1)
        position = iota((rows, taps_b * angles), 0).astype(jnp.float32) - (rows - 1) / 2.0
        spread = slope_wide * position
        tap = lane // angles - half
        line = 0
        for group, ends in enumerate(bands):
            reached = (tap + taps_b * group).astype(jnp.float32)
            hat = jnp.maximum(1.0 - jnp.abs(reached - spread), 0.0)
            if 2 * ends < rows:
                hat = jnp.concatenate([hat[:ends], hat[rows - ends:]], axis=0)
            high, low = split(hat)
            kb_hi[subset, line:line + 2 * ends, :] = high
            kb_lo[subset, line:line + 2 * ends, :] = low
            line += 2 * ends

    for copy in local:
        copy.wait()
    for subset in range(SUBSETS):
        geometry(subset)
    pl.semaphore_wait(barrier, rays + 1)

    for peer in peers:
        x_copy(peer, False).start()
    for copy in held:
        copy.wait()

    for peer in peers:
        a_copy(peer, False).start()
    column = pl.multiple_of(chunk * place, chunk)
    m_all[me] = mv[:, :, pl.ds(column, chunk)]

    start, offset = window(place)
    mine.wait()
    for peer in peers:
        x_copy(peer, True).wait_recv()

    column = iota((1, reach), 1) + place * chunk - LANE
    inside = (column >= 0) & (column < breadth)
    for s in range(slices):
        for p in range(rays):
            part = xin[p, s, :, LANE:LANE + reach]
            xw[s, p * strip:(p + 1) * strip, :] = jnp.where(inside, part, 0.0)

    half_lane = iota((1, LANE), 1) < LANE // 2

    def circle(value):
        edge = jnp.where(half_lane, value[:, reach - LANE:], value[:, :LANE])
        return jnp.concatenate([value[:, LANE:LANE + chunk], edge], axis=1)

    def turn(value, amount):
        amount = amount % value.shape[1]
        return value if amount == 0 else pltpu.roll(value, amount, 1)

    def project(subset, s):
        current = xw[s]
        stacked = jnp.concatenate([turn(current, j) for j in range(taps_f)], axis=0)
        lines = dot2(kf[subset], stacked)
        forward = jnp.zeros((angles, reach), jnp.float32)
        for group in range(kf.shape[1] // angles):
            forward += turn(lines[group * angles:(group + 1) * angles], taps_f * group - half)
        return forward

    def back_project(subset, s, forward, stored):
        residual = circle(jnp.where(inside, stored - forward, 0.0))
        stacked = jnp.concatenate([turn(residual, -j) for j in range(taps_b)], axis=0)
        lines = dot3(kb_hi[subset], kb_lo[subset], stacked)
        blocks = [jnp.zeros((8, ring), jnp.float32) for _ in range(rows // 8)]
        line = 0
        for group, ends in enumerate(bands):
            turned = turn(lines[line:line + 2 * ends], half - taps_b * group)
            line += 2 * ends
            for at in range(2 * ends // 8):
                row = at if at < ends // 8 else at + (rows - 2 * ends) // 8
                blocks[row] = blocks[row] + turned[at * 8:(at + 1) * 8]
        return circle(xw[s]) + jnp.concatenate(blocks, axis=0) / (rows * angles)

    lane = iota((1, ring), 1)
    ring_column = place * chunk + jnp.where(lane < chunk + LANE // 2, lane, lane - ring)
    valid_c = (ring_column >= 0) & (ring_column < breadth - 1)
    valid_r = iota((rows, 1), 0) < rows - 1
    first_slice = cut * slices - 2
    total_slices = slices * cuts

    def tv_pass(source, target, low, high):
        before = None
        for t in range(low - 1, high):
            centre = ext[source, t]
            step_s = ext[source, t + 1] - centre
            at = first_slice + t
            step_s = jnp.where((at >= 0) & (at < total_slices - 1), step_s, 0.0)
            step_r = jnp.where(valid_r, pltpu.roll(centre, rows - 1, 0) - centre, 0.0)
            step_c = jnp.where(valid_c, turn(centre, -1) - centre, 0.0)
            inverse = lax.rsqrt(
                step_s * step_s + step_r * step_r + step_c * step_c + TV_EPS * TV_EPS
            )
            flow_s = step_s * inverse
            if t >= low:
                flow_r = step_r * inverse
                flow_c = step_c * inverse
                spread = flow_s - before
                spread = spread + flow_r - pltpu.roll(flow_r, 1, 0)
                spread = spread + flow_c - turn(flow_c, 1)
                ext[target, t] = centre + TV_STEP * spread
            before = flow_s

    def gather_measured():
        for peer in peers:
            a_copy(peer, True).wait_recv()
        copies = []
        for subset in range(SUBSETS):
            m_mid[subset] = m_all[order_ref[subset]]
            copies.append([
                send(
                    m_mid.at[subset, :, :, pl.ds(at, LANE)], m_edge.at[subset, side],
                    e_send.at[subset, side], e_recv.at[subset, side], (near, cut),
                )
                for side, near, at in ((0, east, chunk - LANE), (1, west, 0))
            ])
            for copy in copies[-1]:
                copy.start()
        return copies

    octets = rows // 8
    pack_lane = iota((1, LANE), 1) // 4

    for subset in range(SUBSETS):
        for s in range(slices):
            forward = project(subset, s)
            if s == 0 and subset == 0:
                edge_copies = gather_measured()
            if s == 0:
                for copy in edge_copies[subset]:
                    copy.wait_recv()
            stored = jnp.concatenate(
                [m_edge[subset, 0, s], m_mid[subset, s], m_edge[subset, 1, s]], axis=1
            )
            ext[0, 2 + s] = back_project(subset, s, forward, stored)
            for side, near in ((0, up), (1, down)):
                send(
                    ext.at[0, 2 + s, :, pl.ds(0, chunk)], zland.at[subset, side, s],
                    z_send.at[subset, side, s], z_recv.at[subset, side, s], (me, near),
                ).start()
        packed = jnp.zeros((8, LANE), jnp.float32)
        for s in range(slices):
            for g in range(octets):
                k = octets * s + g
                edge = ext[0, 2 + s, g * 8:(g + 1) * 8, chunk:]
                packed = jnp.where(pack_lane == k, turn(edge, 2 + 4 * k), packed)
        pack[subset] = packed
        for side, near in ((0, up), (1, down)):
            send(
                pack.at[subset], pland.at[subset, side],
                p_send.at[subset, side], p_recv.at[subset, side], (me, near),
            ).start()
        for side, near in ((0, up), (1, down)):
            for s in range(slices):
                send(
                    ext.at[0, 2 + s, :, pl.ds(0, chunk)], zland.at[subset, side, s],
                    z_send.at[subset, side, s], z_recv.at[subset, side, s], (me, near),
                ).wait()
            send(
                pack.at[subset], pland.at[subset, side],
                p_send.at[subset, side], p_recv.at[subset, side], (me, near),
            ).wait()
            base = (2 + slices) * side
            packed = pland[subset, side]
            for s in range(slices):
                ext[0, base + s, :, :chunk] = zland[subset, side, s]
                for g in range(octets):
                    k = octets * s + g
                    ext[0, base + s, g * 8:(g + 1) * 8, chunk:] = turn(packed, -(2 + 4 * k))
        tv_pass(0, 1, 1, 3 + slices)
        tv_pass(1, 0, 2, 2 + slices)
        if subset < SUBSETS - 1:
            side_copies = [
                send(
                    ext.at[0, pl.ds(2, slices), :, pl.ds(at, LANE)], hland.at[side],
                    h_send.at[side], h_recv.at[side], (near, cut),
                )
                for side, near, at in ((0, east, chunk - LANE), (1, west, 0))
            ]
            for copy in side_copies:
                copy.start()
            for copy in side_copies:
                copy.wait()
            for s in range(slices):
                joined = jnp.concatenate(
                    [hland[0, s], ext[0, 2 + s, :, :chunk], hland[1, s]], axis=1
                )
                xw[s] = jnp.where(inside, joined, 0.0)

    for s in range(slices):
        for p in range(rays):
            obuf[p, s] = ext[0, 2 + s, p * strip:(p + 1) * strip, :chunk]
    for peer in peers:
        o_copy(peer, False).start()
    column = pl.multiple_of(place * chunk, chunk)
    last = pltpu.make_async_copy(obuf.at[me], out_ref.at[:, :, pl.ds(column, chunk)], own_sem.at[2])
    last.start()

    for peer in peers:
        x_copy(peer, False).wait_send()
        a_copy(peer, False).wait_send()
    for copies in edge_copies:
        for copy in copies:
            copy.wait_send()

    for peer in peers:
        o_copy(peer, True).wait_recv()
    for peer in peers:
        o_copy(peer, False).wait_send()
    last.wait()


def on_device(rays, cuts, initial, measured, order, angle_index):
    slices, strip, breadth = initial.shape
    angles = measured.shape[1]
    rows = strip * rays
    chunk = breadth // rays
    reach = chunk + 2 * LANE
    ring = chunk + LANE
    taps_f, taps_b = 4, 8
    groups_f = -(-(rows + 1) // taps_f)
    lines_b = 2 * sum(band_rows(rows, taps_b))
    dma = pltpu.SemaphoreType.DMA
    f32, bf16 = jnp.float32, jnp.bfloat16
    anywhere = pl.BlockSpec(memory_space=pl.ANY)

    return pl.pallas_call(
        functools.partial(kernel, rays, cuts),
        out_shape=jax.ShapeDtypeStruct(initial.shape, f32),
        in_specs=[anywhere] * 4,
        out_specs=anywhere,
        scratch_shapes=[
            pltpu.SMEM(order.shape, jnp.int32),
            pltpu.VMEM(angle_index.shape, jnp.int32),
            pltpu.VMEM((slices, angles, breadth), f32),
            pltpu.VMEM((rays, slices, strip, reach + 2 * LANE), f32),
            pltpu.VMEM((SUBSETS, slices, angles, chunk), f32),
            pltpu.VMEM((rays, slices, angles, chunk), f32),
            pltpu.VMEM((SUBSETS, 2, slices, angles, LANE), f32),
            pltpu.VMEM((slices, rows, reach), f32),
            pltpu.VMEM((SUBSETS, groups_f * angles, taps_f * rows), bf16),
            pltpu.VMEM((SUBSETS, lines_b, taps_b * angles), bf16),
            pltpu.VMEM((SUBSETS, lines_b, taps_b * angles), bf16),
            pltpu.VMEM((2, slices + 4, rows, ring), f32),
            pltpu.VMEM((SUBSETS, 8, LANE), f32),
            pltpu.VMEM((SUBSETS, 2, slices, rows, chunk), f32),
            pltpu.VMEM((SUBSETS, 2, 8, LANE), f32),
            pltpu.VMEM((2, slices, rows, LANE), f32),
            pltpu.VMEM((rays, slices, strip, chunk), f32),
            dma((rays,)), dma((rays,)),
            dma((rays,)), dma((rays,)),
            dma((SUBSETS, 2, slices)), dma((SUBSETS, 2, slices)),
            dma((SUBSETS, 2)), dma((SUBSETS, 2)),
            dma((2,)), dma((2,)),
            dma((SUBSETS, 2)), dma((SUBSETS, 2)),
            dma((rays,)), dma((rays,)),
            dma((3 + slices,)),
        ],
        compiler_params=pltpu.CompilerParams(
            collective_id=0, has_side_effects=True, vmem_limit_bytes=60 * 2**20
        ),
    )(initial, measured, order, angle_index)


def solution(mesh):
    return jax.shard_map(
        functools.partial(on_device, mesh.shape["ray"], mesh.shape["cuts"]),
        mesh=mesh,
        in_specs=(P("cuts", "ray", None), P("ray", None, "cuts", None), P(), P()),
        out_specs=P("cuts", "ray", None),
        check_vma=False,
    )
```

time: 80 us -> 61.3 us (0.77)
  Pallas kernels: 75.6 us -> 59.5 us
  local copies, waits for them, and re-layouts: 4.14 us -> 1.57 us
    pallas_call x1, Pallas kernels: 75.6 us -> 59.5 us  [on_device(): pl.pallas_call(functools.partial(kernel, rays, cuts), out_shape=jax.Shape...]
    unnamed x9 -> x1, local copies, waits for them, and re-layouts: 4.14 us -> 1.57 us
where the time goes in v2:
time: 61.3 us; the launch traced here: 61.1 us
  Pallas kernels  59.5 us (97%)
  local copies, waits for them, and re-layouts  1.57 us (3%)
    pallas_call x1, Pallas kernels, on_device(): pl.pallas_call(functools.partial(kernel, rays, cuts), out_shape=jax.Shape...  59.5 us
    unnamed x1, local copies, waits for them, and re-layouts  1.57 us

profile of v2, /device:TPU:1, one launch (start us, length us, event | category | flops | bytes accessed | tf_op | source)
XLA Modules:
  0.0 61.1 jit_solution(15973752663562348425)
XLA Ops:
  0.0 59.5 %shard_map.46 = f32[2,4,4096]{2,1,0:T(4,128)} custom-call(f32[2,4,4096]{2,1,0:T(4,128)} %init_ref.1, f32[1,32,2,4096]{3,2,1,0:T(2,128)} %meas_ref.1, s32[16]{0:T(128)} %order_in.1, s32[16,32]{1,0:T(8,128)} %angle_in.1), custom_call_target="tpu_custom_call" | custom-call | tf_op jit(solution)/shard_map/pallas_call | solution.py:401
  59.6 1.6 %copy.6 = f32[2,4,4096]{2,1,0:T(4,128)} copy(f32[2,4,4096]{2,1,0:T(4,128)} %shard_map.46) | data formatting | bytes 262144

commit v3 on v2

--- a/solution.py
+++ b/solution.py
@@ -69,9 +69,9 @@
 def kernel(
     rays, cuts,
     init_ref, meas_ref, order_in, angle_in, out_ref,
-    order_ref, angle_ref, mv, xin, m_mid, m_all, m_edge, xw, kf, kb_hi, kb_lo,
+    order_ref, angle_ref, mv, m_mate, m_pick, xin, m_mid, m_all0, m_all1, m_edge, xw, kf, kb_hi, kb_lo,
     ext, pack, zland, pland, hland, obuf,
-    x_send, x_recv, a_send, a_recv, z_send, z_recv, p_send, p_recv,
+    x_send, x_recv, t_send, t_recv, a_send, a_recv, z_send, z_recv, p_send, p_recv,
     h_send, h_recv, e_send, e_recv, o_send, o_recv, own_sem,
 ):
     slices, strip, breadth = init_ref.shape
@@ -86,6 +86,10 @@
     up, down = lax.rem(cut + 1, cuts), lax.rem(cut + cuts - 1, cuts)
     east, west = ray_of(lax.rem(place + 1, rays)), ray_of(lax.rem(place + rays - 1, rays))
     peers = [partner(me, mask) for mask in FAR_FIRST]
+    core, mate = me % 2, partner(me, 1)
+    alike = [partner(me, mask) for mask in FAR_FIRST if mask % 2 == 0]
+    m_all = (m_all0, m_all1)
+    pairs = rays // 2
 
     barrier = pltpu.get_barrier_semaphore()
     for peer in peers:
@@ -130,12 +134,19 @@
             x_send.at[peer], x_recv.at[origin], (peer, cut),
         )
 
-    def a_copy(peer, arriving):
-        column = pl.multiple_of(chunk * (place if arriving else chunk_of(peer)), chunk)
+    def mate_copy(pair):
+        theirs = pl.multiple_of(chunk * (2 * pair + 1 - core), chunk)
+        return send(
+            mv.at[:, :, pl.ds(theirs, chunk)], m_mate.at[pair],
+            t_send.at[pair], t_recv.at[pair], (mate, cut),
+        )
+
+    def a_copy(subset, peer, arriving):
         origin = peer if arriving else me
         return send(
-            mv.at[:, :, pl.ds(column, chunk)], m_all.at[origin],
-            a_send.at[peer], a_recv.at[origin], (peer, cut),
+            m_pick.at[subset, (place if arriving else chunk_of(peer)) // 2],
+            m_all[subset].at[origin // 2],
+            a_send.at[subset, peer // 2], a_recv.at[subset, origin // 2], (peer, cut),
         )
 
     def o_copy(peer, arriving):
@@ -191,15 +202,24 @@
         geometry(subset)
     pl.semaphore_wait(barrier, rays + 1)
 
-    for peer in peers:
-        x_copy(peer, False).start()
     for copy in held:
         copy.wait()
-
-    for peer in peers:
-        a_copy(peer, False).start()
-    column = pl.multiple_of(chunk * place, chunk)
-    m_all[me] = mv[:, :, pl.ds(column, chunk)]
+    for pair in range(pairs):
+        mate_copy(pair).start()
+    for peer in peers:
+        x_copy(peer, False).start()
+    for pair in range(pairs):
+        mate_copy(pair).wait_recv()
+    def hand_on(subset):
+        ours = order_ref[subset] == me
+        for pair in range(pairs):
+            column = pl.multiple_of(chunk * (2 * pair + core), chunk)
+            m_pick[subset, pair] = jnp.where(ours, mv[:, :, pl.ds(column, chunk)], m_mate[pair])
+        for peer in alike:
+            a_copy(subset, peer, False).start()
+        m_all[subset][me // 2] = m_pick[subset, place // 2]
+
+    hand_on(0)
 
     start, offset = window(place)
     mine.wait()
@@ -275,21 +295,19 @@
                 ext[target, t] = centre + TV_STEP * spread
             before = flow_s
 
-    def gather_measured():
-        for peer in peers:
-            a_copy(peer, True).wait_recv()
-        copies = []
-        for subset in range(SUBSETS):
-            m_mid[subset] = m_all[order_ref[subset]]
-            copies.append([
-                send(
-                    m_mid.at[subset, :, :, pl.ds(at, LANE)], m_edge.at[subset, side],
-                    e_send.at[subset, side], e_recv.at[subset, side], (near, cut),
-                )
-                for side, near, at in ((0, east, chunk - LANE), (1, west, 0))
-            ])
-            for copy in copies[-1]:
-                copy.start()
+    def gather_measured(subset):
+        for peer in alike:
+            a_copy(subset, peer, True).wait_recv()
+        m_mid[subset] = m_all[subset][order_ref[subset] // 2]
+        copies = [
+            send(
+                m_mid.at[subset, :, :, pl.ds(at, LANE)], m_edge.at[subset, side],
+                e_send.at[subset, side], e_recv.at[subset, side], (near, cut),
+            )
+            for side, near, at in ((0, east, chunk - LANE), (1, west, 0))
+        ]
+        for copy in copies:
+            copy.start()
         return copies
 
     octets = rows // 8
@@ -299,7 +317,8 @@
         for s in range(slices):
             forward = project(subset, s)
             if s == 0 and subset == 0:
-                edge_copies = gather_measured()
+                edge_copies = [gather_measured(subset)]
+                hand_on(1)
             if s == 0:
                 for copy in edge_copies[subset]:
                     copy.wait_recv()
@@ -353,6 +372,7 @@
             ]
             for copy in side_copies:
                 copy.start()
+            edge_copies.append(gather_measured(subset + 1))
             for copy in side_copies:
                 copy.wait()
             for s in range(slices):
@@ -372,7 +392,11 @@
 
     for peer in peers:
         x_copy(peer, False).wait_send()
-        a_copy(peer, False).wait_send()
+    for pair in range(pairs):
+        mate_copy(pair).wait_send()
+    for subset in range(SUBSETS):
+        for peer in alike:
+            a_copy(subset, peer, False).wait_send()
     for copies in edge_copies:
         for copy in copies:
             copy.wait_send()
@@ -407,9 +431,12 @@
             pltpu.SMEM(order.shape, jnp.int32),
             pltpu.VMEM(angle_index.shape, jnp.int32),
             pltpu.VMEM((slices, angles, breadth), f32),
+            pltpu.VMEM((rays // 2, slices, angles, chunk), f32),
+            pltpu.VMEM((SUBSETS, rays // 2, slices, angles, chunk), f32),
             pltpu.VMEM((rays, slices, strip, reach + 2 * LANE), f32),
             pltpu.VMEM((SUBSETS, slices, angles, chunk), f32),
-            pltpu.VMEM((rays, slices, angles, chunk), f32),
+            pltpu.VMEM((rays // 2, slices, angles, chunk), f32),
+            pltpu.VMEM((rays // 2, slices, angles, chunk), f32),
             pltpu.VMEM((SUBSETS, 2, slices, angles, LANE), f32),
             pltpu.VMEM((slices, rows, reach), f32),
             pltpu.VMEM((SUBSETS, groups_f * angles, taps_f * rows), bf16),
@@ -422,7 +449,8 @@
             pltpu.VMEM((2, slices, rows, LANE), f32),
             pltpu.VMEM((rays, slices, strip, chunk), f32),
             dma((rays,)), dma((rays,)),
-            dma((rays,)), dma((rays,)),
+            dma((rays // 2,)), dma((rays // 2,)),
+            dma((SUBSETS, rays // 2)), dma((SUBSETS, rays // 2)),
             dma((SUBSETS, 2, slices)), dma((SUBSETS, 2, slices)),
             dma((SUBSETS, 2)), dma((SUBSETS, 2)),
             dma((2,)), dma((2,)),

time: 61.3 us -> 56.1 us (0.915)
  Pallas kernels: 59.5 us -> 54.4 us
    pallas_call x1, Pallas kernels: 59.5 us -> 54.4 us  [on_device(): pl.pallas_call(functools.partial(kernel, rays, cuts), out_shape=jax.Shape...]
where the time goes in v3:
time: 56.1 us; the launch traced here: 56 us
  Pallas kernels  54.4 us (97%)
  local copies, waits for them, and re-layouts  1.57 us (3%)
    pallas_call x1, Pallas kernels, on_device(): pl.pallas_call(functools.partial(kernel, rays, cuts), out_shape=jax.Shape...  54.4 us
    unnamed x1, local copies, waits for them, and re-layouts  1.57 us

profile of v3, /device:TPU:1, one launch (start us, length us, event | category | flops | bytes accessed | tf_op | source)
XLA Modules:
  0.0 56.0 jit_solution(1601474417140674218)
XLA Ops:
  0.0 54.4 %shard_map.46 = f32[2,4,4096]{2,1,0:T(4,128)} custom-call(f32[2,4,4096]{2,1,0:T(4,128)} %init_ref.1, f32[1,32,2,4096]{3,2,1,0:T(2,128)} %meas_ref.1, s32[16]{0:T(128)} %order_in.1, s32[16,32]{1,0:T(8,128)} %angle_in.1), custom_call_target="tpu_custom_call" | custom-call | tf_op jit(solution)/shard_map/pallas_call | solution.py:425
  54.4 1.6 %copy.6 = f32[2,4,4096]{2,1,0:T(4,128)} copy(f32[2,4,4096]{2,1,0:T(4,128)} %shard_map.46) | data formatting | bytes 262144

commit v4 on v3

--- a/solution.py
+++ b/solution.py
@@ -70,7 +70,7 @@
     rays, cuts,
     init_ref, meas_ref, order_in, angle_in, out_ref,
     order_ref, angle_ref, mv, m_mate, m_pick, xin, m_mid, m_all0, m_all1, m_edge, xw, kf, kb_hi, kb_lo,
-    ext, pack, zland, pland, hland, obuf,
+    ext, pack, pland, hland, obuf,
     x_send, x_recv, t_send, t_recv, a_send, a_recv, z_send, z_recv, p_send, p_recv,
     h_send, h_recv, e_send, e_recv, o_send, o_recv, own_sem,
 ):
@@ -83,7 +83,9 @@
     me = lax.axis_index("ray")
     cut = lax.axis_index("cuts")
     place = chunk_of(me)
-    up, down = lax.rem(cut + 1, cuts), lax.rem(cut + cuts - 1, cuts)
+    up, down = jnp.minimum(cut + 1, cuts - 1), jnp.maximum(cut - 1, 0)
+    has_up, has_down = cut < cuts - 1, cut > 0
+    sides = ((0, up, has_up, has_down), (1, down, has_down, has_up))
     east, west = ray_of(lax.rem(place + 1, rays)), ray_of(lax.rem(place + rays - 1, rays))
     peers = [partner(me, mask) for mask in FAR_FIRST]
     core, mate = me % 2, partner(me, 1)
@@ -94,8 +96,10 @@
     barrier = pltpu.get_barrier_semaphore()
     for peer in peers:
         pl.semaphore_signal(barrier, inc=1, device_id=(peer, cut), device_id_type=MESH)
-    for near in (up, down):
-        pl.semaphore_signal(barrier, inc=1, device_id=(me, near), device_id_type=MESH)
+    for _, near, there, _ in sides:
+        @pl.when(there)
+        def _(near=near):
+            pl.semaphore_signal(barrier, inc=1, device_id=(me, near), device_id_type=MESH)
 
     def window(spot):
         start = jnp.clip(spot * chunk - LANE, 0, breadth - reach)
@@ -196,29 +200,40 @@
             kb_lo[subset, line:line + 2 * ends, :] = low
             line += 2 * ends
 
+    for side, _, _, comes in sides:
+        @pl.when(jnp.logical_not(comes))
+        def _(side=side):
+            for subset in range(SUBSETS):
+                for s in range(slices):
+                    ext[2 * subset, (2 + slices) * side + s] = jnp.zeros((rows, ring), jnp.float32)
+                pland[subset, side] = jnp.zeros((8, LANE), jnp.float32)
+
     for copy in local:
         copy.wait()
     for subset in range(SUBSETS):
         geometry(subset)
-    pl.semaphore_wait(barrier, rays + 1)
+    pl.semaphore_wait(barrier, rays - 1 + has_up.astype(jnp.int32) + has_down.astype(jnp.int32))
 
     for copy in held:
         copy.wait()
-    for pair in range(pairs):
+    spots = [chunk_of(peer) // 2 for peer in alike] + [place // 2]
+    for pair in spots:
         mate_copy(pair).start()
-    for peer in peers:
-        x_copy(peer, False).start()
-    for pair in range(pairs):
-        mate_copy(pair).wait_recv()
     def hand_on(subset):
         ours = order_ref[subset] == me
-        for pair in range(pairs):
+        for pair, peer in zip(spots, [*alike, None]):
+            if subset == 0:
+                mate_copy(pair).wait_recv()
             column = pl.multiple_of(chunk * (2 * pair + core), chunk)
-            m_pick[subset, pair] = jnp.where(ours, mv[:, :, pl.ds(column, chunk)], m_mate[pair])
-        for peer in alike:
-            a_copy(subset, peer, False).start()
-        m_all[subset][me // 2] = m_pick[subset, place // 2]
-
+            picked = jnp.where(ours, mv[:, :, pl.ds(column, chunk)], m_mate[pair])
+            if peer is None:
+                m_all[subset][me // 2] = picked
+            else:
+                m_pick[subset, pair] = picked
+                a_copy(subset, peer, False).start()
+
+    for peer in peers:
+        x_copy(peer, False).start()
     hand_on(0)
 
     start, offset = window(place)
@@ -273,8 +288,9 @@
     first_slice = cut * slices - 2
     total_slices = slices * cuts
 
-    def tv_pass(source, target, low, high):
+    def tv_pass(source, target, low, high, hand_sideways=False):
         before = None
+        copies = []
         for t in range(low - 1, high):
             centre = ext[source, t]
             step_s = ext[source, t + 1] - centre
@@ -293,7 +309,15 @@
                 spread = spread + flow_r - pltpu.roll(flow_r, 1, 0)
                 spread = spread + flow_c - turn(flow_c, 1)
                 ext[target, t] = centre + TV_STEP * spread
+                if hand_sideways:
+                    for side, near, at in ((0, east, chunk - LANE), (1, west, 0)):
+                        copies.append(send(
+                            ext.at[target, t, :, pl.ds(at, LANE)], hland.at[side, t - low],
+                            h_send.at[side, t - low], h_recv.at[side, t - low], (near, cut),
+                        ))
+                        copies[-1].start()
             before = flow_s
+        return copies
 
     def gather_measured(subset):
         for peer in alike:
@@ -310,12 +334,35 @@
             copy.start()
         return copies
 
+    def z_copy(subset, side, s):
+        return send(
+            ext.at[2 * subset, 2 + s, :, pl.ds(0, chunk)],
+            ext.at[2 * subset, (2 + slices) * side + s, :, pl.ds(0, chunk)],
+            z_send.at[subset, side, s], z_recv.at[subset, side, s], (me, sides[side][1]),
+        )
+
+    def p_copy(subset, side):
+        return send(
+            pack.at[subset], pland.at[subset, side],
+            p_send.at[subset, side], p_recv.at[subset, side], (me, sides[side][1]),
+        )
+
     octets = rows // 8
     pack_lane = iota((1, LANE), 1) // 4
 
+    ahead = [project(0, s) for s in range(slices)]
     for subset in range(SUBSETS):
         for s in range(slices):
-            forward = project(subset, s)
+            if subset == 0:
+                forward = ahead[s]
+            else:
+                for copy in side_copies[2 * s:2 * s + 2]:
+                    copy.wait()
+                joined = jnp.concatenate(
+                    [hland[0, s], ext[3, 2 + s, :, :chunk], hland[1, s]], axis=1
+                )
+                xw[s] = jnp.where(inside, joined, 0.0)
+                forward = project(subset, s)
             if s == 0 and subset == 0:
                 edge_copies = [gather_measured(subset)]
                 hand_on(1)
@@ -325,65 +372,41 @@
             stored = jnp.concatenate(
                 [m_edge[subset, 0, s], m_mid[subset, s], m_edge[subset, 1, s]], axis=1
             )
-            ext[0, 2 + s] = back_project(subset, s, forward, stored)
-            for side, near in ((0, up), (1, down)):
-                send(
-                    ext.at[0, 2 + s, :, pl.ds(0, chunk)], zland.at[subset, side, s],
-                    z_send.at[subset, side, s], z_recv.at[subset, side, s], (me, near),
-                ).start()
+            ext[2 * subset, 2 + s] = back_project(subset, s, forward, stored)
+            for side, _, there, _ in sides:
+                @pl.when(there)
+                def _(side=side, s=s):
+                    z_copy(subset, side, s).start()
         packed = jnp.zeros((8, LANE), jnp.float32)
         for s in range(slices):
             for g in range(octets):
                 k = octets * s + g
-                edge = ext[0, 2 + s, g * 8:(g + 1) * 8, chunk:]
+                edge = ext[2 * subset, 2 + s, g * 8:(g + 1) * 8, chunk:]
                 packed = jnp.where(pack_lane == k, turn(edge, 2 + 4 * k), packed)
         pack[subset] = packed
-        for side, near in ((0, up), (1, down)):
-            send(
-                pack.at[subset], pland.at[subset, side],
-                p_send.at[subset, side], p_recv.at[subset, side], (me, near),
-            ).start()
-        for side, near in ((0, up), (1, down)):
-            for s in range(slices):
-                send(
-                    ext.at[0, 2 + s, :, pl.ds(0, chunk)], zland.at[subset, side, s],
-                    z_send.at[subset, side, s], z_recv.at[subset, side, s], (me, near),
-                ).wait()
-            send(
-                pack.at[subset], pland.at[subset, side],
-                p_send.at[subset, side], p_recv.at[subset, side], (me, near),
-            ).wait()
+        for side, _, there, _ in sides:
+            @pl.when(there)
+            def _(side=side):
+                p_copy(subset, side).start()
+        for side, _, there, comes in sides:
+            @pl.when(comes)
+            def _(side=side):
+                for s in range(slices):
+                    z_copy(subset, side, s).wait_recv()
+                p_copy(subset, side).wait_recv()
             base = (2 + slices) * side
             packed = pland[subset, side]
             for s in range(slices):
-                ext[0, base + s, :, :chunk] = zland[subset, side, s]
                 for g in range(octets):
                     k = octets * s + g
-                    ext[0, base + s, g * 8:(g + 1) * 8, chunk:] = turn(packed, -(2 + 4 * k))
-        tv_pass(0, 1, 1, 3 + slices)
-        tv_pass(1, 0, 2, 2 + slices)
+                    ext[2 * subset, base + s, g * 8:(g + 1) * 8, chunk:] = turn(packed, -(2 + 4 * k))
+        tv_pass(2 * subset, 1, 1, 3 + slices)
+        side_copies = tv_pass(1, 3, 2, 2 + slices, subset < SUBSETS - 1)
         if subset < SUBSETS - 1:
-            side_copies = [
-                send(
-                    ext.at[0, pl.ds(2, slices), :, pl.ds(at, LANE)], hland.at[side],
-                    h_send.at[side], h_recv.at[side], (near, cut),
-                )
-                for side, near, at in ((0, east, chunk - LANE), (1, west, 0))
-            ]
-            for copy in side_copies:
-                copy.start()
             edge_copies.append(gather_measured(subset + 1))
-            for copy in side_copies:
-                copy.wait()
-            for s in range(slices):
-                joined = jnp.concatenate(
-                    [hland[0, s], ext[0, 2 + s, :, :chunk], hland[1, s]], axis=1
-                )
-                xw[s] = jnp.where(inside, joined, 0.0)
-
     for s in range(slices):
         for p in range(rays):
-            obuf[p, s] = ext[0, 2 + s, p * strip:(p + 1) * strip, :chunk]
+            obuf[p, s] = ext[3, 2 + s, p * strip:(p + 1) * strip, :chunk]
     for peer in peers:
         o_copy(peer, False).start()
     column = pl.multiple_of(place * chunk, chunk)
@@ -400,12 +423,26 @@
     for copies in edge_copies:
         for copy in copies:
             copy.wait_send()
+    for side, _, there, _ in sides:
+        @pl.when(there)
+        def _(side=side):
+            for subset in range(SUBSETS):
+                for s in range(slices):
+                    z_copy(subset, side, s).wait_send()
+                p_copy(subset, side).wait_send()
+
 
     for peer in peers:
         o_copy(peer, True).wait_recv()
     for peer in peers:
         o_copy(peer, False).wait_send()
     last.wait()
+
+
+def pass_on(source, target, sem):
+    copy = pltpu.make_async_copy(source, target, sem.at[0])
+    copy.start()
+    copy.wait()
 
 
 def on_device(rays, cuts, initial, measured, order, angle_index):
@@ -422,7 +459,7 @@
     f32, bf16 = jnp.float32, jnp.bfloat16
     anywhere = pl.BlockSpec(memory_space=pl.ANY)
 
-    return pl.pallas_call(
+    gathered = pl.pallas_call(
         functools.partial(kernel, rays, cuts),
         out_shape=jax.ShapeDtypeStruct(initial.shape, f32),
         in_specs=[anywhere] * 4,
@@ -442,9 +479,8 @@
             pltpu.VMEM((SUBSETS, groups_f * angles, taps_f * rows), bf16),
             pltpu.VMEM((SUBSETS, lines_b, taps_b * angles), bf16),
             pltpu.VMEM((SUBSETS, lines_b, taps_b * angles), bf16),
-            pltpu.VMEM((2, slices + 4, rows, ring), f32),
+            pltpu.VMEM((4, slices + 4, rows, ring), f32),
             pltpu.VMEM((SUBSETS, 8, LANE), f32),
-            pltpu.VMEM((SUBSETS, 2, slices, rows, chunk), f32),
             pltpu.VMEM((SUBSETS, 2, 8, LANE), f32),
             pltpu.VMEM((2, slices, rows, LANE), f32),
             pltpu.VMEM((rays, slices, strip, chunk), f32),
@@ -453,7 +489,7 @@
             dma((SUBSETS, rays // 2)), dma((SUBSETS, rays // 2)),
             dma((SUBSETS, 2, slices)), dma((SUBSETS, 2, slices)),
             dma((SUBSETS, 2)), dma((SUBSETS, 2)),
-            dma((2,)), dma((2,)),
+            dma((2, slices)), dma((2, slices)),
             dma((SUBSETS, 2)), dma((SUBSETS, 2)),
             dma((rays,)), dma((rays,)),
             dma((3 + slices,)),
@@ -462,6 +498,7 @@
             collective_id=0, has_side_effects=True, vmem_limit_bytes=60 * 2**20
         ),
     )(initial, measured, order, angle_index)
+    return gathered
 
 
 def solution(mesh):

time: 56.1 us -> 53.3 us (0.950)
  the two profiles are of different devices: /device:TPU:1 before, /device:TPU:3 now
where the time goes in v4:
time: 53.3 us; the launch traced here: 53.2 us
  Pallas kernels  51.6 us (97%)
  local copies, waits for them, and re-layouts  1.57 us (3%)
    pallas_call x1, Pallas kernels, on_device(): pl.pallas_call(functools.partial(kernel, rays, cuts), out_shape=jax.Shape...  51.6 us
    unnamed x1, local copies, waits for them, and re-layouts  1.57 us

profile of v4, /device:TPU:3, one launch (start us, length us, event | category | flops | bytes accessed | tf_op | source)
XLA Modules:
  0.0 53.2 jit_solution(1530561688761448865)
XLA Ops:
  0.0 51.6 %shard_map.46 = f32[2,4,4096]{2,1,0:T(4,128)} custom-call(f32[2,4,4096]{2,1,0:T(4,128)} %init_ref.1, f32[1,32,2,4096]{3,2,1,0:T(2,128)} %meas_ref.1, s32[16]{0:T(128)} %order_in.1, s32[16,32]{1,0:T(8,128)} %angle_in.1), custom_call_target="tpu_custom_call" | custom-call | tf_op jit(solution)/shard_map/pallas_call | solution.py:462
  51.6 1.6 %copy.6 = f32[2,4,4096]{2,1,0:T(4,128)} copy(f32[2,4,4096]{2,1,0:T(4,128)} %shard_map.46) | data formatting | bytes 262144

commit v5 on v4

--- a/solution.py
+++ b/solution.py
@@ -210,8 +210,6 @@
 
     for copy in local:
         copy.wait()
-    for subset in range(SUBSETS):
-        geometry(subset)
     pl.semaphore_wait(barrier, rays - 1 + has_up.astype(jnp.int32) + has_down.astype(jnp.int32))
 
     for copy in held:
@@ -235,6 +233,8 @@
     for peer in peers:
         x_copy(peer, False).start()
     hand_on(0)
+    for subset in range(SUBSETS):
+        geometry(subset)
 
     start, offset = window(place)
     mine.wait()

time: 53.3 us -> 53.3 us (level)
  no operation moved by 1% of the time
where the time goes in v5:
time: 53.3 us; the launch traced here: 53.2 us
  Pallas kernels  51.6 us (97%)
  local copies, waits for them, and re-layouts  1.57 us (3%)
    pallas_call x1, Pallas kernels, on_device(): pl.pallas_call(functools.partial(kernel, rays, cuts), out_shape=jax.Shape...  51.6 us
    unnamed x1, local copies, waits for them, and re-layouts  1.57 us

profile of v5, /device:TPU:3, one launch (start us, length us, event | category | flops | bytes accessed | tf_op | source)
XLA Modules:
  0.0 53.2 jit_solution(7140403995081524856)
XLA Ops:
  0.0 51.6 %shard_map.46 = f32[2,4,4096]{2,1,0:T(4,128)} custom-call(f32[2,4,4096]{2,1,0:T(4,128)} %init_ref.1, f32[1,32,2,4096]{3,2,1,0:T(2,128)} %meas_ref.1, s32[16]{0:T(128)} %order_in.1, s32[16,32]{1,0:T(8,128)} %angle_in.1), custom_call_target="tpu_custom_call" | custom-call | tf_op jit(solution)/shard_map/pallas_call | solution.py:462
  51.6 1.6 %copy.6 = f32[2,4,4096]{2,1,0:T(4,128)} copy(f32[2,4,4096]{2,1,0:T(4,128)} %shard_map.46) | data formatting | bytes 262144
